TPU v7x, 512 devices: a whole 4x8x8 slice. The times are simulated.
512 devices in a mesh: layer: 4 (over x), seq: 16 (over y, core), tile: 8 (over z).
Axes of the slice: x: 4, y: 8, z: 8, core: 2. Of those that a mesh axis runs over, the one named last changes fastest.
Arguments:
- activations: bfloat16 [16, 3072, 4096], P('layer', 'seq', 'tile'), parts along dimension 0, may hold values from -6 to 6
- out_grads: bfloat16 [16, 3072, 14336], P('layer', 'seq', 'tile'), parts along dimension 0, may hold values from -6 to 6
- proj_in: bfloat16 [16384, 128], P(('layer', 'tile')), parts along dimension 0, may hold values from -0.09375 to 0.09375
- proj_out: bfloat16 [57344, 256], P(('layer', 'tile')), parts along dimension 0, may hold values from -0.046875 to 0.046875
- seq_lengths: int32 [4], replicated, may hold values from 1 to 3072, 7680 in all
- tile_map: int32 [128, 2], replicated, may hold values from 0 to 127, as said below
- prior_cov: float32 [512, 256, 256], P(('layer', 'seq', 'tile')), parts along dimension 0, may hold values from -6 to 6
Outputs:
- covariance: float32 [512, 256, 256], P(('layer', 'seq', 'tile')), parts along dimension 0
There are 4 independent parts, one for each index of `layer`. A program takes and returns all parts, laid end to end along the dimension named above; an argument that names none is the same for every part. Nothing has to cross between parts.
Inputs may be any that keep to these rules, and one draw needn't show every extreme that they name: `tile_map`: each row holds two feature block numbers, the first not above the second; rows may repeat.
All inputs are finite; a program needn't handle non-finite values.
Results may differ from a plain program's by a relative error of at most 0.0003.
Values sent between devices are 32-bit elements; how exact they have to be, the bound alone decides.
No kernel may reach another device: no remote copies, remote signals or barrier semaphores. Data moves between devices by JAX's collectives and lax.ppermute only.
A program may use at most 192 MiB of HBM per device.

v0:
```python
import jax
import jax.numpy as jnp
from jax import lax
from jax.sharding import PartitionSpec as P


def project_tokens(act_rows, grad_rows, proj_in, proj_out):
    left_side = jnp.einsum("slc,ck->lsk", act_rows, proj_in, preferred_element_type=jnp.float32)
    right_side = jnp.einsum("slc,ck->lsk", grad_rows, proj_out, preferred_element_type=jnp.float32)
    return jnp.concatenate([left_side, right_side], axis=2)


def body(activations, out_grads, proj_in, proj_out, seq_lengths, tile_map, prior_cov):
    tiles_here = prior_cov.shape[0]
    block_size = prior_cov.shape[1]
    seq_count = activations.shape[0]
    tok_len = activations.shape[1]
    width_in = proj_in.shape[1]
    width_out = proj_out.shape[1]
    tile_count = lax.axis_size("tile")
    tok_rows = tok_len // tile_count
    whole_term = project_tokens(activations, out_grads, proj_in, proj_out)
    totals = lax.psum(whole_term, "tile")
    summed = lax.dynamic_slice_in_dim(totals, lax.axis_index("tile") * tok_rows, tok_rows, 0)
    positions = (
        lax.axis_index("seq") * tok_len
        + lax.axis_index("tile") * tok_rows
        + jnp.arange(tok_rows, dtype=jnp.int32)
    )
    token_mask = (positions[:, None] < seq_lengths[None, :]).astype(jnp.float32)
    token_weight = token_mask * lax.rsqrt(seq_lengths.astype(jnp.float32))[None, :]
    left_part = summed[:, :, :width_in]
    right_part = summed[:, :, width_in:] * token_weight[:, :, None]
    partial_value = jnp.einsum(
        "lsj,lsi->sji", right_part, left_part, precision=lax.Precision.HIGHEST
    )
    partial_value = partial_value.reshape(seq_count, width_out * width_in)
    offsets = jnp.arange(block_size, dtype=jnp.int32)
    features = lax.psum_scatter(partial_value, ("seq", "tile"), scatter_dimension=1, tiled=True)
    owner_index = lax.axis_index(("seq", "tile"))
    own_pairs = lax.dynamic_slice_in_dim(tile_map, owner_index * tiles_here, tiles_here, 0)
    shard_piece = lax.all_gather(features, ("seq", "tile"), axis=1, tiled=True)
    piece_width = shard_piece.shape[1]
    columns = own_pairs[:, :, None] * block_size + offsets
    inside = (columns >= 0) & (columns < piece_width)
    picked = jnp.take(shard_piece, jnp.clip(columns, 0, piece_width - 1), axis=1)
    picked = jnp.where(inside[None], picked, 0.0)
    chosen = jnp.transpose(picked, (1, 2, 0, 3))
    product = jnp.einsum(
        "kse,ksf->kef", chosen[:, 0], chosen[:, 1], precision=lax.Precision.HIGHEST
    )
    return prior_cov + product


def solution(mesh):
    return jax.shard_map(
        body,
        mesh=mesh,
        in_specs=(
            P("layer", "seq", "tile"),
            P("layer", "seq", "tile"),
            P(("layer", "tile"), None),
            P(("layer", "tile"), None),
            P(),
            P(),
            P(("layer", "seq", "tile"), None, None),
        ),
        out_specs=P(("layer", "seq", "tile"), None, None),
        check_vma=False,
    )
```

profile of v0, /device:TPU:25, one launch (start us, length us, event | category | flops | bytes accessed | tf_op | source)
XLA Modules:
  0.0 484.0 jit_solution(7159621079205856472)
XLA Ops:
  6.5 0.0 copy-start
  6.5 1.8 copy-done
  8.3 2.1 convolution_bitcast_fusion
  10.4 0.0 copy-done.1
  10.4 0.0 copy-done.3
  10.4 0.4 convolution_bitcast_fusion.1
  10.8 1.1 pad_maximum_fusion
  11.9 0.0 all-reduce.2.cloned.1.call-update
  12.0 0.0 reduce-scatter.2.cloned.1.call-start
  12.0 0.6 copy-done.5
  12.6 0.1 compare_select_fusion.2
  12.7 82.7 %all-reduce.2.cloned.1.call-done = f32[192,4,384]{2,0,1:T(8,128)} async-done(((f32[192,4,384]{2,0,1:T(8,128)}), f32[192,4,384]{2,0,1:T(8,128)}) %all-reduce.2.cloned.1.call-update) | async-done | bytes 1179664 | tf_op jit(solution)/shard_map/psum | solution.py:23
  95.4 2.0 fusion.3
  97.4 8.7 %copy.10 = f32[4,256,128]{0,2,1:T(8,128)} copy(f32[4,256,128]{2,1,0:T(8,128)S(1)} %fusion.3) | data formatting | bytes 1048576 | tf_op jit(solution)/shard_map/reshape | solution.py:37
  106.1 0.0 reduce-scatter.2.cloned.1.call-update
  106.1 0.6 copy-done.4
  106.7 0.2 multiply_reduce_fusion
  106.9 0.1 fusion.6
  107.0 0.1 compare_and_fusion.1
  107.1 220.6 %reduce-scatter.2.cloned.1.call-done = f32[4,256]{0,1:T(8,128)} async-done(((f32[4,32768]{0,1:T(8,128)}), f32[4,256]{0,1:T(8,128)}) %reduce-scatter.2.cloned.1.call-update) | async-done | bytes 4112 | tf_op jit(solution)/shard_map/reduce_scatter | solution.py:39
  327.7 141.3 %all_gather.3 = f32[4,32768]{0,1:T(8,128)} all-gather(f32[4,256]{0,1:T(8,128)} %reduce-scatter.2.cloned.1.call-done), channel_id=1, replica_groups=mesh['layer'=4,'seq'=16,'tile'=8] {'seq','tile'}, dimensions={1}, use_global_device_ids=true | all-gather | bytes 528384 | tf_op jit(solution)/shard_map/all_gather | solution.py:42
  469.0 6.8 %gather_fusion = f32[512,4]{1,0:T(8,128)S(1)} fusion(f32[4,32768]{0,1:T(8,128)} %all_gather.3, s32[1024]{0:T(1024)S(1)} %pad_clamp_fusion), kind=kCustom, calls=%fused_computation | custom fusion | bytes 18432 | tf_op jit(solution)/shard_map/jit(_take)/gather | solution.py:46
  475.8 0.2 select_bitcast_fusion
  476.0 1.1 fusion
  (11 shorter events, 0.0 us)
Async XLA Ops:
  6.5 1.8 copy-start
  6.5 3.9 copy-start.1
  6.5 88.8 %all-reduce.2.cloned.1.call-start = ((), (), s32[]{:S(2)}) async-start(), calls=%async_computation.1 | async-start | bytes 2359296 | tf_op jit(solution)/shard_map/psum | solution.py:23
  8.3 2.1 copy-start.3
  11.9 0.7 copy-start.5
  12.0 315.8 %reduce-scatter.2.cloned.1.call-start = ((), (), s32[]{:S(2)}) async-start(), calls=%async_computation.2 | async-start | bytes 16908288 | tf_op jit(solution)/shard_map/reduce_scatter | solution.py:39
  106.1 0.7 copy-start.4
  107.1 368.9 %copy-start.2 = (f32[1,256,256]{2,1,0:T(8,128)S(1)}, f32[1,256,256]{2,1,0:T(8,128)}, u32[]{:S(2)}) copy-start(f32[1,256,256]{2,1,0:T(8,128)} %param.13) | copy-start | bytes 786436
Sparse Core Ops, SparseCore 0:
  12.1 83.2 all-reduce.1
  106.2 221.4 reduce-scatter.1
where the time goes:
time: 484 us
  waiting for transfers between devices  303 us (63%)
  blocking collectives  141 us (29%)
  local copies, waits for them, and re-layouts  18.5 us (4%)
  between operations  13.5 us (3%)
  matrix products  5.57 us (1%)
    reduce_scatter x1, waiting for transfers between devices, body(): lax.psum_scatter(partial_value, ('seq', 'tile'), scatter_dimension=1, til...  221 us
    all_gather x1, blocking collectives, body(): shard_piece = lax.all_gather(features, ('seq', 'tile'), axis=1, tiled=True)  141 us
    psum x1, waiting for transfers between devices, body(): totals = lax.psum(whole_term, 'tile')  82.7 us
  transfers between devices with their start and end apart: 2, of which 2 were waited for; matrix products, arithmetic and copies ran while one was open for 0% of the time, Pallas kernels for 0%

commit v1 on v0

--- a/solution.py
+++ b/solution.py
@@ -20,7 +20,11 @@
     tile_count = lax.axis_size("tile")
     tok_rows = tok_len // tile_count
     whole_term = project_tokens(activations, out_grads, proj_in, proj_out)
-    totals = lax.psum(whole_term, "tile")
+    peers = lax.axis_size("tile")
+    totals, stride = (whole_term, 1)
+    while stride < peers:
+        totals = totals + lax.ppermute(totals, "tile", [(i, i ^ stride) for i in range(peers)])
+        stride = 2 * stride
     summed = lax.dynamic_slice_in_dim(totals, lax.axis_index("tile") * tok_rows, tok_rows, 0)
     positions = (
         lax.axis_index("seq") * tok_len

time: 484 us -> 546 us (1.13)
  the two profiles are of different devices: /device:TPU:25 before, /device:TPU:2 now
where the time goes in v1:
time: 546 us; the launch traced here: 545 us
  waiting for transfers between devices  351 us (64%)
  blocking collectives  137 us (25%)
  starting transfers between devices  18.8 us (3%)
  local copies, waits for them, and re-layouts  17.9 us (3%)
  between operations  13.5 us (2%)
    reduce_scatter x1, waiting for transfers between devices, body(): lax.psum_scatter(partial_value, ('seq', 'tile'), scatter_dimension=1, til...  223 us
    all_gather x1, blocking collectives, body(): shard_piece = lax.all_gather(features, ('seq', 'tile'), axis=1, tiled=True)  137 us
    ppermute x3, waiting for transfers between devices, body(): lax.ppermute(totals, 'tile', [(i, i ^ stride) for i in range(peers)])  128 us
    ppermute x3, starting transfers between devices, body(): lax.ppermute(totals, 'tile', [(i, i ^ stride) for i in range(peers)])  18.8 us
  transfers between devices with their start and end apart: 4, of which 4 were waited for; matrix products, arithmetic and copies ran while one was open for 0% of the time, Pallas kernels for 0%

profile of v1, /device:TPU:2, one launch (start us, length us, event | category | flops | bytes accessed | tf_op | source)
XLA Modules:
  0.0 545.4 jit_solution(15329065363934360973)
XLA Ops:
  6.5 1.8 copy-done
  8.3 2.1 convolution_bitcast_fusion
  10.4 0.4 convolution_bitcast_fusion.1
  10.8 0.1 pad_maximum_fusion
  10.9 4.3 collective-permute-start
  15.2 26.0 %collective-permute-done = f32[192,4,384]{2,0,1:T(8,128)S(1)} collective-permute-done((f32[192,4,384]{2,0,1:T(8,128)S(1)}, f32[192,4,384]{2,0,1:T(8,128)S(1)}, u32[]{:S(2)}, u32[]{:S(2)}) %collective-permute-start) | collective-permute-done | bytes 1179680 | tf_op jit(solution)/shard_map/ppermute | solution.py:26
  41.1 0.1 fusion.7
  41.3 6.1 %collective-permute-start.1 = (f32[192,4,384]{2,0,1:T(8,128)S(1)}, f32[192,4,384]{2,0,1:T(8,128)S(1)}, u32[]{:S(2)}, u32[]{:S(2)}) collective-permute-start(f32[192,4,384]{2,0,1:T(8,128)S(1)} %fusion.7), channel_id=1, source_target_pairs={{0,2},{1,3},{2,0},{3,1},{4,6},{5,7},{6,4},{7,5},{8,10},{9,11},{10,... | collective-permute-start | bytes 3538952 | tf_op jit(solution)/shard_map/ppermute | solution.py:26
  47.4 50.7 %collective-permute-done.1 = f32[192,4,384]{2,0,1:T(8,128)S(1)} collective-permute-done((f32[192,4,384]{2,0,1:T(8,128)S(1)}, f32[192,4,384]{2,0,1:T(8,128)S(1)}, u32[]{:S(2)}, u32[]{:S(2)}) %collective-permute-start.1) | collective-permute-done | bytes 1179680 | tf_op jit(solution)/shard_map/ppermute | solution.py:26
  98.1 1.1 add.109
  99.2 8.4 %collective-permute-start.2 = (f32[192,4,384]{2,0,1:T(8,128)}, f32[192,4,384]{2,0,1:T(8,128)}, u32[]{:S(2)}, u32[]{:S(2)}) collective-permute-start(f32[192,4,384]{2,0,1:T(8,128)} %add.109), channel_id=1, source_target_pairs={{0,4},{1,5},{2,6},{3,7},{4,0},{5,1},{6,2},{7,3},{8,12},{9,13},{10,... | collective-permute-start | bytes 3538952 | tf_op jit(solution)/shard_map/ppermute | solution.py:26
  107.7 51.1 %collective-permute-done.2 = f32[192,4,384]{2,0,1:T(8,128)} collective-permute-done((f32[192,4,384]{2,0,1:T(8,128)}, f32[192,4,384]{2,0,1:T(8,128)}, u32[]{:S(2)}, u32[]{:S(2)}) %collective-permute-start.2) | collective-permute-done | bytes 1179680 | tf_op jit(solution)/shard_map/ppermute | solution.py:26
  158.8 1.0 dynamic-slice_add_fusion
  159.8 1.1 fusion.3
  161.0 8.7 %copy.10 = f32[4,256,128]{0,2,1:T(8,128)} copy(f32[4,256,128]{2,1,0:T(8,128)S(1)} %fusion.3) | data formatting | bytes 1048576 | tf_op jit(solution)/shard_map/reshape | solution.py:41
  169.7 0.6 copy-done.4
  170.3 0.2 multiply_reduce_fusion
  170.5 0.1 fusion.6
  170.6 0.1 compare_and_fusion.1
  170.7 222.9 %reduce-scatter.2.cloned.1.call-done = f32[4,256]{0,1:T(8,128)} async-done(((f32[4,32768]{0,1:T(8,128)}), f32[4,256]{0,1:T(8,128)}) %reduce-scatter.2.cloned.1.call-update) | async-done | bytes 4112 | tf_op jit(solution)/shard_map/reduce_scatter | solution.py:43
  393.6 136.8 %all_gather.3 = f32[4,32768]{0,1:T(8,128)} all-gather(f32[4,256]{0,1:T(8,128)} %reduce-scatter.2.cloned.1.call-done), channel_id=1, replica_groups=mesh['layer'=4,'seq'=16,'tile'=8] {'seq','tile'}, dimensions={1}, use_global_device_ids=true | all-gather | bytes 528384 | tf_op jit(solution)/shard_map/all_gather | solution.py:46
  530.4 6.8 %gather_fusion = f32[512,4]{1,0:T(8,128)S(1)} fusion(f32[4,32768]{0,1:T(8,128)} %all_gather.3, s32[1024]{0:T(1024)S(1)} %pad_clamp_fusion), kind=kCustom, calls=%fused_computation | custom fusion | bytes 18432 | tf_op jit(solution)/shard_map/jit(_take)/gather | solution.py:50
  537.3 0.2 select_bitcast_fusion
  537.5 1.1 fusion
  (17 shorter events, 0.1 us)
Async XLA Ops:
  6.5 1.8 copy-start
  6.5 3.9 copy-start.1
  6.5 387.1 %reduce-scatter.2.cloned.1.call-start = ((), (), s32[]{:S(2)}) async-start(), calls=%async_computation.1 | async-start | bytes 16908288 | tf_op jit(solution)/shard_map/reduce_scatter | solution.py:43
  8.3 2.1 copy-start.3
  10.9 30.2 %collective-permute-start = (f32[192,4,384]{2,0,1:T(8,128)S(1)}, f32[192,4,384]{2,0,1:T(8,128)S(1)}, u32[]{:S(2)}, u32[]{:S(2)}) collective-permute-start(f32[192,4,384]{2,0,1:T(8,128)S(1)} %pad_maximum_fusion), channel_id=1, source_target_pairs={{0,1},{1,0},{2,3},{3,2},{4,5},{5,4},{6,7},{7,6},{8,9},{9,8},{10,11... | collective-permute-start | bytes 3538952 | tf_op jit(solution)/shard_map/ppermute | solution.py:26
  41.3 66.4 %copy-start.5 = (s32[4]{0:T(128)S(1)}, s32[4]{0:T(128)}, u32[]{:S(2)}) copy-start(s32[4]{0:T(128)} %param.11) | copy-start | bytes 52
  41.3 56.8 %collective-permute-start.1 = (f32[192,4,384]{2,0,1:T(8,128)S(1)}, f32[192,4,384]{2,0,1:T(8,128)S(1)}, u32[]{:S(2)}, u32[]{:S(2)}) collective-permute-start(f32[192,4,384]{2,0,1:T(8,128)S(1)} %fusion.7), channel_id=1, source_target_pairs={{0,2},{1,3},{2,0},{3,1},{4,6},{5,7},{6,4},{7,5},{8,10},{9,11},{10,... | collective-permute-start | bytes 3538952 | tf_op jit(solution)/shard_map/ppermute | solution.py:26
  99.2 59.6 %collective-permute-start.2 = (f32[192,4,384]{2,0,1:T(8,128)}, f32[192,4,384]{2,0,1:T(8,128)}, u32[]{:S(2)}, u32[]{:S(2)}) collective-permute-start(f32[192,4,384]{2,0,1:T(8,128)} %add.109), channel_id=1, source_target_pairs={{0,4},{1,5},{2,6},{3,7},{4,0},{5,1},{6,2},{7,3},{8,12},{9,13},{10,... | collective-permute-start | bytes 3538952 | tf_op jit(solution)/shard_map/ppermute | solution.py:26
  169.7 0.7 copy-start.4
  170.7 366.8 %copy-start.2 = (f32[1,256,256]{2,1,0:T(8,128)S(1)}, f32[1,256,256]{2,1,0:T(8,128)}, u32[]{:S(2)}) copy-start(f32[1,256,256]{2,1,0:T(8,128)} %param.13) | copy-start | bytes 786436
Sparse Core Ops, SparseCore 0:
  169.8 223.7 reduce-scatter.1
